TPU v7x, 512 devices: a whole 4x4x16 slice. The times are simulated.
512 devices in a mesh: row: 32 (over y, x, core), col: 16 (over z).
Axes of the slice: x: 4, y: 4, z: 16, core: 2. Of those that a mesh axis runs over, the one named last changes fastest.
Arguments:
- iterate_t: bfloat16 [32, 16, 64, 32768], P(None, 'col', None, 'row'), may hold values from -0.03125 to 0.03125
- vectors: bfloat16 [32768, 256], P(('row', 'col')), may hold values from -6 to 6
- old_factor_t: bfloat16 [512, 32768], P('col', 'row'), may hold values from -5 to 5
Outputs:
- panel: float32 [32768, 256], P(('row', 'col'))
- basis: float32 [768, 32768], P('col', 'row')
All inputs are finite; a program needn't handle non-finite values.
Results may differ from a plain program's by a relative error of at most 0.0013.
Values may be sent and summed in bfloat16 or wider, within the bound.
A program may use at most 64 MiB of HBM per device.

v0:
```python
import jax
import jax.numpy as jnp
from jax import lax
from jax.sharding import PartitionSpec as P

NSTATE = 32768


def body(iterate_t, vectors, old_factor_t):
    flat_iterate = iterate_t.reshape(-1, iterate_t.shape[-1])
    highest = lax.Precision.HIGHEST

    def apply_iterate(vector):
        gathered = lax.all_gather(vector, "row", axis=0, tiled=True)
        return lax.psum_scatter(
            lax.dot_general(
                flat_iterate, gathered, (((0,), (0,)), ((), ())), preferred_element_type=jnp.float32
            ),
            "col",
            scatter_dimension=0,
            tiled=True,
        )

    first_full = apply_iterate(vectors)
    second = apply_iterate(first_full.astype(jnp.bfloat16)).astype(jnp.bfloat16)
    panel = 1.5 * first_full - 0.5 * apply_iterate(second)
    old_gathered = lax.all_gather(old_factor_t, "col", axis=0, tiled=True)
    panel_gathered = lax.all_gather(panel, "col", axis=0, tiled=True)
    old_full = old_gathered.astype(jnp.float32)
    scale_gram = 1.0 / NSTATE
    column = lax.axis_index("col")
    groups = lax.axis_size("col")
    panel_share = panel.shape[1] // groups
    own_panel = lax.dynamic_slice_in_dim(panel_gathered, column * panel_share, panel_share, 1)
    own_old = old_factor_t.astype(jnp.float32)
    old_columns = (
        jnp.concatenate(
            [
                lax.dot_general(
                    old_gathered,
                    old_factor_t,
                    (((1,), (1,)), ((), ())),
                    preferred_element_type=jnp.float32,
                ),
                lax.dot_general(
                    panel_gathered, own_old, (((0,), (1,)), ((), ())), precision=highest
                ),
            ],
            0,
        )
        * scale_gram
    )
    panel_columns = (
        jnp.concatenate(
            [
                jnp.dot(old_full, own_panel, precision=highest),
                lax.dot_general(
                    panel_gathered, own_panel, (((0,), (0,)), ((), ())), precision=highest
                ),
            ],
            0,
        )
        * scale_gram
    )
    summed_old, summed_panel = lax.psum((old_columns, panel_columns), "row")
    left_part, right_part = (
        lax.all_gather(summed_old, "col", axis=1, tiled=True),
        lax.all_gather(summed_panel, "col", axis=1, tiled=True),
    )
    gram = jnp.concatenate([left_part, right_part], 1)
    lower_factor = jnp.linalg.cholesky(gram)
    identity = jnp.eye(gram.shape[0], dtype=jnp.float32)
    inverse = jax.scipy.linalg.solve_triangular(lower_factor, identity, lower=True)
    basis_share = gram.shape[0] // groups
    inverse_rows = lax.dynamic_slice_in_dim(inverse, column * basis_share, basis_share, 0)
    old_count = old_gathered.shape[0]
    basis = jnp.dot(inverse_rows[:, :old_count], old_full, precision=highest)
    basis = basis + lax.dot_general(
        inverse_rows[:, old_count:], panel_gathered, (((1,), (1,)), ((), ())), precision=highest
    )
    return (panel, basis)


def solution(mesh):
    return jax.shard_map(
        body,
        mesh=mesh,
        in_specs=(P(None, "col", None, "row"), P(("row", "col"), None), P("col", "row")),
        out_specs=(P(("row", "col"), None), P("col", "row")),
        check_vma=False,
    )
```

profile of v0, /device:TPU:32, one launch (start us, length us, event | category | flops | bytes accessed | tf_op | source)
XLA Modules:
  0.0 1116.8 jit_solution(5605788853649218226)
XLA Ops:
  7.9 65.4 %all-gather.7.cloned.1.call-done = bf16[2048,256]{1,0:T(8,128)(2,1)} async-done(((bf16[64,256]{1,0:T(8,128)(2,1)}), bf16[2048,256]{1,0:T(8,128)(2,1)}) %all-gather.7.cloned.1.call-update) | async-done | bytes 1048592 | tf_op jit(solution)/shard_map/all_gather | solution.py:14
  73.4 4.7 fusion.64
  78.2 69.4 %reduce-scatter.6.cloned.1.call-done = f32[64,256]{1,0:T(8,128)} async-done(((f32[1024,256]{1,0:T(8,128)}), f32[64,256]{1,0:T(8,128)}) %reduce-scatter.6.cloned.1.call-update) | async-done | bytes 65552 | tf_op jit(solution)/shard_map/reduce_scatter | solution.py:15
  149.1 59.0 %all-gather.9.cloned.1.call-done = bf16[2048,256]{1,0:T(8,128)(2,1)} async-done(((bf16[64,256]{1,0:T(8,128)(2,1)}), bf16[2048,256]{1,0:T(8,128)(2,1)}) %all-gather.9.cloned.1.call-update) | async-done | bytes 1048592 | tf_op jit(solution)/shard_map/all_gather | solution.py:14
  208.1 3.8 convolution_bitcast_fusion.1
  213.3 69.4 %reduce-scatter.10.cloned.1.call-done = f32[64,256]{1,0:T(8,128)} async-done(((f32[1024,256]{1,0:T(8,128)}), f32[64,256]{1,0:T(8,128)}) %reduce-scatter.10.cloned.1.call-update) | async-done | bytes 65552 | tf_op jit(solution)/shard_map/reduce_scatter | solution.py:15
  284.2 58.4 %all-gather.11.cloned.1.call-done = bf16[2048,256]{1,0:T(8,128)(2,1)} async-done(((bf16[64,256]{1,0:T(8,128)(2,1)}), bf16[2048,256]{1,0:T(8,128)(2,1)}) %all-gather.11.cloned.1.call-update) | async-done | bytes 1048592 | tf_op jit(solution)/shard_map/all_gather | solution.py:14
  342.6 5.3 convolution_bitcast_fusion
  348.7 68.6 %reduce-scatter.8.cloned.1.call-done = f32[64,256]{1,0:T(8,128)} async-done(((f32[1024,256]{1,0:T(8,128)}), f32[64,256]{1,0:T(8,128)}) %reduce-scatter.8.cloned.1.call-update) | async-done | bytes 65552 | tf_op jit(solution)/shard_map/reduce_scatter | solution.py:15
  418.9 70.0 %all-gather.13.cloned.1.call-done = bf16[512,1024]{1,0:T(8,128)(2,1)} async-done(((bf16[32,1024]{1,0:T(8,128)(2,1)}), bf16[512,1024]{1,0:T(8,128)(2,1)}) %all-gather.13.cloned.1.call-update) | async-done | bytes 1048592 | tf_op jit(solution)/shard_map/all_gather | solution.py:27
  490.5 69.3 %all-gather.15.cloned.1.call-done = f32[1024,256]{1,0:T(8,128)} async-done(((f32[64,256]{1,0:T(8,128)}), f32[1024,256]{1,0:T(8,128)}) %all-gather.15.cloned.1.call-update) | async-done | bytes 1048592 | tf_op jit(solution)/shard_map/all_gather | solution.py:28
  562.3 127.3 %all-reduce.3.cloned.1.call-done = f32[768,32]{0,1:T(8,128)} async-done(((f32[768,32]{0,1:T(8,128)}), f32[768,32]{0,1:T(8,128)}) %all-reduce.3.cloned.1.call-update) | async-done | bytes 98320 | tf_op jit(solution)/shard_map/psum | solution.py:65
  694.5 125.5 %psum.15 = f32[768,16]{0,1:T(8,128)S(1)} all-reduce(f32[768,16]{0,1:T(8,128)S(1)} %maximum_multiply_fusion.1), channel_id=1, replica_groups=mesh['row'=32,'col'=16] {'row'}, use_global_device_ids=true, to_apply=%region_4.0 | all-reduce | flops 12288 | bytes 98304 | tf_op jit(solution)/shard_map/psum | solution.py:65
  820.0 36.1 %all_gather.27 = f32[768,256]{0,1:T(8,128)} all-gather(f32[768,16]{0,1:T(8,128)S(1)} %psum.15), channel_id=1, replica_groups=mesh['row'=32,'col'=16] {'col'}, dimensions={1}, use_global_device_ids=true | all-gather | bytes 835584 | tf_op jit(solution)/shard_map/all_gather | solution.py:68
  863.4 11.7 %cholesky.165 = f32[128,128]{1,0:T(8,128)S(1)} custom-call(f32[128,128]{1,0:T(8,128)S(1)} %cholesky.424), custom_call_target="Cholesky" | custom-call | tf_op jit(solution)/shard_map/jit(cholesky)/cholesky | solution.py:71
  875.1 9.8 custom-call.47
  888.6 11.7 %cholesky.188 = f32[128,128]{1,0:T(8,128)S(1)} custom-call(f32[128,128]{1,0:T(8,128)S(1)} %cholesky.428), custom_call_target="Cholesky" | custom-call | tf_op jit(solution)/shard_map/jit(cholesky)/cholesky | solution.py:71
  900.4 10.0 custom-call.48
  913.9 11.7 %cholesky.354 = f32[128,128]{1,0:T(8,128)S(1)} custom-call(f32[128,128]{1,0:T(8,128)S(1)} %cholesky.433), custom_call_target="Cholesky" | custom-call | tf_op jit(solution)/shard_map/jit(cholesky)/cholesky | solution.py:71
  926.3 9.8 custom-call.49
  939.6 12.1 %cholesky.373 = f32[128,128]{1,0:T(8,128)S(1)} custom-call(f32[128,128]{1,0:T(8,128)S(1)} %cholesky.438), custom_call_target="Cholesky" | custom-call | tf_op jit(solution)/shard_map/jit(cholesky)/cholesky | solution.py:71
  952.5 9.8 custom-call.50
  965.6 13.2 %cholesky.392 = f32[128,128]{1,0:T(8,128)} custom-call(f32[128,128]{1,0:T(8,128)} %cholesky.443), custom_call_target="Cholesky" | custom-call | tf_op jit(solution)/shard_map/jit(cholesky)/cholesky | solution.py:71
  980.9 11.3 %custom-call.51 = f32[1,128,128]{1,2,0:T(8,128)} custom-call(f32[1,128,128]{2,1,0:T(8,128)} %get-tuple-element.33), custom_call_target="InvertDiagBlocksLowerTriangular" | custom-call | tf_op jit(solution)/shard_map/jit(cholesky)/cholesky | solution.py:71
  994.6 11.9 %cholesky.410 = f32[128,128]{1,0:T(8,128)S(1)} custom-call(f32[128,128]{1,0:T(8,128)S(1)} %convolution_subtract_fusion.8), custom_call_target="Cholesky" | custom-call | tf_op jit(solution)/shard_map/jit(cholesky)/cholesky | solution.py:71
  1013.2 20.6 %while.1 = (s32[]{:T(128)}, f32[768,768]{1,0:T(8,128)}, s32[6,2]{0,1:T(2,128)S(1)}, f32[6,128,128]{2,1,0:T(8,128)}, s32[]{:T(128)}) while((s32[]{:T(128)}, f32[768,768]{1,0:T(8,128)}, s32[6,2]{0,1:T(2,128)S(1)}, f32[6,128,128]{2,1,0:T(8,128)}, s32[]{:T(128)}) %tuple.44), condition=%wide.while_cond, body=%wide.while_body.sunk | while | flops 2 | bytes 132705 | solution.py:73
  1013.8 2.9 bitcast_dynamic-update-slice_fusion.2
  1017.4 2.8 bitcast_dynamic-update-slice_fusion.2
  1020.8 2.8 bitcast_dynamic-update-slice_fusion.2
  1024.2 2.8 bitcast_dynamic-update-slice_fusion.2
  1027.7 2.8 bitcast_dynamic-update-slice_fusion.2
  1033.9 60.4 %custom-call.52 = f32[6,128,128]{1,2,0:T(8,128)} custom-call(f32[6,128,128]{2,1,0:T(8,128)} %get-tuple-element.9), custom_call_target="InvertDiagBlocksLowerTriangular" | custom-call | tf_op jit(solution)/shard_map/jit(_solve_triangular)/triangular_solve | solution.py:73
  (118 shorter events, 68.5 us)
Async XLA Ops:
  7.2 66.2 %all-gather.7.cloned.1.call-start = ((), (), s32[]{:S(2)}) async-start(), calls=%async_computation.3 | async-start | bytes 1081344 | tf_op jit(solution)/shard_map/all_gather | solution.py:14
  7.9 139.6 %reduce-scatter.6.cloned.1.call-start = ((), (), s32[]{:S(2)}) async-start(), calls=%async_computation.4 | async-start | bytes 1114112 | tf_op jit(solution)/shard_map/reduce_scatter | solution.py:15
  78.1 130.0 %all-gather.9.cloned.1.call-start = ((), (), s32[]{:S(2)}) async-start(), calls=%async_computation.5 | async-start | bytes 1081344 | tf_op jit(solution)/shard_map/all_gather | solution.py:14
  149.0 133.7 %reduce-scatter.10.cloned.1.call-start = ((), (), s32[]{:S(2)}) async-start(), calls=%async_computation.12 | async-start | bytes 1114112 | tf_op jit(solution)/shard_map/reduce_scatter | solution.py:15
  213.2 129.4 %all-gather.11.cloned.1.call-start = ((), (), s32[]{:S(2)}) async-start(), calls=%async_computation.6 | async-start | bytes 1081344 | tf_op jit(solution)/shard_map/all_gather | solution.py:14
  284.2 133.2 %copy-start.11 = (f32[64,256]{1,0:T(8,128)S(1)}, f32[64,256]{1,0:T(8,128)}, u32[]{:S(2)}) copy-start(f32[64,256]{1,0:T(8,128)} %reduce-scatter.6.cloned.1.call-done) | copy-start | bytes 196612
  284.2 204.7 %copy-start.9 = (bf16[32,1024]{1,0:T(8,128)(2,1)S(1)}, bf16[32,1024]{1,0:T(8,128)(2,1)}, u32[]{:S(2)}) copy-start(bf16[32,1024]{1,0:T(8,128)(2,1)} %param.5) | copy-start | bytes 196612
  284.2 133.1 %reduce-scatter.8.cloned.1.call-start = ((), (), s32[]{:S(2)}) async-start(), calls=%async_computation.7 | async-start | bytes 1114112 | tf_op jit(solution)/shard_map/reduce_scatter | solution.py:15
  347.9 141.0 %all-gather.13.cloned.1.call-start = ((), (), s32[]{:S(2)}) async-start(), calls=%async_computation.8 | async-start | bytes 1114112 | tf_op jit(solution)/shard_map/all_gather | solution.py:27
  348.7 211.1 %all-gather.15.cloned.1.call-start = ((), (), s32[]{:S(2)}) async-start(), calls=%async_computation.9 | async-start | bytes 1114112 | tf_op jit(solution)/shard_map/all_gather | solution.py:28
  418.8 270.7 %all-reduce.3.cloned.1.call-start = ((), (), s32[]{:S(2)}) async-start(), calls=%async_computation.10 | async-start | bytes 196608 | tf_op jit(solution)/shard_map/psum | solution.py:65
  559.8 132.4 %copy-start = (f32[1024,256]{1,0:T(8,128)S(1)}, f32[1024,256]{1,0:T(8,128)}, u32[]{:S(2)}) copy-start(f32[1024,256]{1,0:T(8,128)} %all-gather.15.cloned.1.call-done) | copy-start | bytes 3145732
  561.6 131.8 %copy-start.1 = (bf16[512,1024]{1,0:T(8,128)(2,1)S(1)}, bf16[512,1024]{1,0:T(8,128)(2,1)}, u32[]{:S(2)}) copy-start(bf16[512,1024]{1,0:T(8,128)(2,1)} %all-gather.13.cloned.1.call-done) | copy-start | bytes 3145732
  562.3 293.9 %all-gather.17.cloned.1.call-start = ((), (), s32[]{:S(2)}) async-start(), calls=%async_computation.11 | async-start | bytes 1671168 | tf_op jit(solution)/shard_map/all_gather | solution.py:67
  856.1 1.6 copy-start.5
  861.9 1.5 copy-start.4
  887.9 0.7 copy-start.6
  913.2 0.7 copy-start.7
  938.9 0.7 copy-start.8
  1013.2 84.4 %copy-start.3 = (f32[768,768]{1,0:T(8,128)S(1)}, f32[768,768]{1,0:T(8,128)}, u32[]{:S(2)}) copy-start(f32[768,768]{1,0:T(8,128)} %fusion.20) | copy-start | bytes 7077892
  1094.2 2.8 copy-start.10
  1104.0 3.4 copy-start.2
Sparse Core Ops, SparseCore 0:
  11.1 62.1 all-gather.6
  78.2 69.2 reduce-scatter.5
  151.7 56.3 all-gather.8
  213.4 69.2 reduce-scatter.9
  286.2 56.3 all-gather.10
  348.0 69.2 reduce-scatter.7
  419.6 69.2 all-gather.12
  491.7 67.9 all-gather.14
  564.0 125.5 all-reduce.2
  691.5 71.4 all-gather.16
where the time goes:
time: 1120 us
  waiting for transfers between devices  658 us (59%)
  other arithmetic  200 us (18%)
  blocking collectives  162 us (14%)
  matrix products  48.3 us (4%)
  local copies, waits for them, and re-layouts  30.1 us (3%)
  between operations  18.5 us (2%)
    reduce_scatter x3, waiting for transfers between devices, apply_iterate(): lax.psum_scatter(lax.dot_general(flat_iterate, gathered, (((0,), (0,)), (...  207 us
    all_gather x3, waiting for transfers between devices, apply_iterate(): gathered = lax.all_gather(vector, 'row', axis=0, tiled=True)  183 us
    another operation x22, other arithmetic, body(): lower_factor = jnp.linalg.cholesky(gram)  128 us
    psum x1, waiting for transfers between devices, body(): summed_old, summed_panel = lax.psum((old_columns, panel_columns), 'row')  127 us
    psum x1, blocking collectives, body(): summed_old, summed_panel = lax.psum((old_columns, panel_columns), 'row')  125 us
    all_gather x1, waiting for transfers between devices, body(): old_gathered = lax.all_gather(old_factor_t, 'col', axis=0, tiled=True)  70 us
    all_gather x1, waiting for transfers between devices, body(): panel_gathered = lax.all_gather(panel, 'col', axis=0, tiled=True)  69.3 us
    another operation x3, other arithmetic, body(): jax.scipy.linalg.solve_triangular(lower_factor, identity, lower=True)  62 us
  transfers between devices with their start and end apart: 10, of which 9 were waited for; matrix products, arithmetic and copies ran while one was open for 1% of the time, Pallas kernels for 0%

commit v1 on v0

--- a/solution.py
+++ b/solution.py
@@ -11,7 +11,9 @@
     highest = lax.Precision.HIGHEST
 
     def apply_iterate(vector):
-        gathered = lax.all_gather(vector, "row", axis=0, tiled=True)
+        gathered = jnp.concatenate(
+            lax.all_to_all(jnp.stack([vector] * lax.axis_size("row")), "row", 0, 0), axis=0
+        )
         return lax.psum_scatter(
             lax.dot_general(
                 flat_iterate, gathered, (((0,), (0,)), ((), ())), preferred_element_type=jnp.float32

time: 1120 us -> 1010 us (0.902)
  waiting for transfers between devices: 658 us -> 466 us
  blocking collectives: 162 us -> 235 us
    all_gather x3 -> x0, waiting for transfers between devices: 183 us -> none  [apply_iterate(): gathered = lax.all_gather(vector, 'row', axis=0, tiled=True)]
    all_to_all x0 -> x3, blocking collectives: none -> 72.9 us  [apply_iterate(): lax.all_to_all(jnp.stack([vector] * lax.axis_size('row')), 'row', 0, 0)]
    another operation x18 -> x21, local copies, waits for them, and re-layouts: 20.6 us -> 22.6 us
  transfers between devices with their start and end apart: 10 -> 7, of which waited for: 9 -> 6; matrix products, arithmetic and copies ran while one was open for 1% -> 1% of each run, Pallas kernels for 0% -> 0%
where the time goes in v1:
time: 1010 us; the launch traced here: 997 us
  waiting for transfers between devices  466 us (46%)
  blocking collectives  235 us (23%)
  other arithmetic  198 us (20%)
  matrix products  47.5 us (5%)
  local copies, waits for them, and re-layouts  32.1 us (3%)
  between operations  18.6 us (2%)
    reduce_scatter x3, waiting for transfers between devices, apply_iterate(): lax.psum_scatter(lax.dot_general(flat_iterate, gathered, (((0,), (0,)), (...  199 us
    another operation x22, other arithmetic, body(): lower_factor = jnp.linalg.cholesky(gram)  128 us
    psum x1, waiting for transfers between devices, body(): summed_old, summed_panel = lax.psum((old_columns, panel_columns), 'row')  127 us
    psum x1, blocking collectives, body(): summed_old, summed_panel = lax.psum((old_columns, panel_columns), 'row')  125 us
    all_to_all x3, blocking collectives, apply_iterate(): lax.all_to_all(jnp.stack([vector] * lax.axis_size('row')), 'row', 0, 0)  72.9 us
    all_gather x1, waiting for transfers between devices, body(): old_gathered = lax.all_gather(old_factor_t, 'col', axis=0, tiled=True)  69.8 us
    all_gather x1, waiting for transfers between devices, body(): panel_gathered = lax.all_gather(panel, 'col', axis=0, tiled=True)  69 us
    another operation x3, other arithmetic, body(): jax.scipy.linalg.solve_triangular(lower_factor, identity, lower=True)  62 us
  transfers between devices with their start and end apart: 7, of which 6 were waited for; matrix products, arithmetic and copies ran while one was open for 1% of the time, Pallas kernels for 0%

profile of v1, /device:TPU:32, one launch (start us, length us, event | category | flops | bytes accessed | tf_op | source)
XLA Modules:
  0.0 997.2 jit_solution(3665384153753884899)
XLA Ops:
  8.1 24.5 %all_to_all.15 = bf16[32,64,256]{2,1,0:T(8,128)(2,1)S(1)} all-to-all(bf16[32,64,256]{2,1,0:T(8,128)(2,1)S(1)} %stack.6), channel_id=1, replica_groups=mesh['row'=32,'col'=16] {'row'}, dimensions={0} | all-to-all | bytes 2097152 | tf_op jit(solution)/shard_map/all_to_all | solution.py:15
  32.5 4.5 fusion.64
  37.1 70.3 %reduce-scatter.6.cloned.1.call-done = f32[64,256]{1,0:T(8,128)} async-done(((f32[1024,256]{1,0:T(8,128)}), f32[64,256]{1,0:T(8,128)}) %reduce-scatter.6.cloned.1.call-update) | async-done | bytes 65552 | tf_op jit(solution)/shard_map/reduce_scatter | solution.py:17
  108.4 24.2 %all_to_all.16 = bf16[32,64,256]{2,1,0:T(8,128)(2,1)S(1)} all-to-all(bf16[32,64,256]{2,1,0:T(8,128)(2,1)S(1)} %stack.7), channel_id=1, replica_groups=mesh['row'=32,'col'=16] {'row'}, dimensions={0} | all-to-all | bytes 2097152 | tf_op jit(solution)/shard_map/all_to_all | solution.py:15
  132.6 3.5 convolution_bitcast_fusion.1
  137.5 64.7 %reduce-scatter.10.cloned.1.call-done = f32[64,256]{1,0:T(8,128)} async-done(((f32[1024,256]{1,0:T(8,128)}), f32[64,256]{1,0:T(8,128)}) %reduce-scatter.10.cloned.1.call-update) | async-done | bytes 65552 | tf_op jit(solution)/shard_map/reduce_scatter | solution.py:17
  203.1 24.3 %all_to_all.17 = bf16[32,64,256]{2,1,0:T(8,128)(2,1)S(1)} all-to-all(bf16[32,64,256]{2,1,0:T(8,128)(2,1)S(1)} %stack.8), channel_id=1, replica_groups=mesh['row'=32,'col'=16] {'row'}, dimensions={0} | all-to-all | bytes 2097152 | tf_op jit(solution)/shard_map/all_to_all | solution.py:15
  227.4 5.0 convolution_bitcast_fusion
  233.1 64.1 %reduce-scatter.8.cloned.1.call-done = f32[64,256]{1,0:T(8,128)} async-done(((f32[1024,256]{1,0:T(8,128)}), f32[64,256]{1,0:T(8,128)}) %reduce-scatter.8.cloned.1.call-update) | async-done | bytes 65552 | tf_op jit(solution)/shard_map/reduce_scatter | solution.py:17
  298.7 69.8 %all-gather.4.cloned.1.call-done = bf16[512,1024]{1,0:T(8,128)(2,1)} async-done(((bf16[32,1024]{1,0:T(8,128)(2,1)}), bf16[512,1024]{1,0:T(8,128)(2,1)}) %all-gather.4.cloned.1.call-update) | async-done | bytes 1048592 | tf_op jit(solution)/shard_map/all_gather | solution.py:29
  370.2 69.0 %all-gather.6.cloned.1.call-done = f32[1024,256]{1,0:T(8,128)} async-done(((f32[64,256]{1,0:T(8,128)}), f32[1024,256]{1,0:T(8,128)}) %all-gather.6.cloned.1.call-update) | async-done | bytes 1048592 | tf_op jit(solution)/shard_map/all_gather | solution.py:30
  441.8 127.1 %all-reduce.3.cloned.1.call-done = f32[768,32]{0,1:T(8,128)} async-done(((f32[768,32]{0,1:T(8,128)}), f32[768,32]{0,1:T(8,128)}) %all-reduce.3.cloned.1.call-update) | async-done | bytes 98320 | tf_op jit(solution)/shard_map/psum | solution.py:67
  573.8 125.5 %psum.15 = f32[768,16]{0,1:T(8,128)S(1)} all-reduce(f32[768,16]{0,1:T(8,128)S(1)} %maximum_multiply_fusion.1), channel_id=1, replica_groups=mesh['row'=32,'col'=16] {'row'}, use_global_device_ids=true, to_apply=%region_4.0 | all-reduce | flops 12288 | bytes 98304 | tf_op jit(solution)/shard_map/psum | solution.py:67
  699.3 36.1 %all_gather.15 = f32[768,256]{0,1:T(8,128)} all-gather(f32[768,16]{0,1:T(8,128)S(1)} %psum.15), channel_id=1, replica_groups=mesh['row'=32,'col'=16] {'col'}, dimensions={1}, use_global_device_ids=true | all-gather | bytes 835584 | tf_op jit(solution)/shard_map/all_gather | solution.py:70
  742.6 11.7 %cholesky.165 = f32[128,128]{1,0:T(8,128)S(1)} custom-call(f32[128,128]{1,0:T(8,128)S(1)} %cholesky.424), custom_call_target="Cholesky" | custom-call | tf_op jit(solution)/shard_map/jit(cholesky)/cholesky | solution.py:73
  754.4 9.8 custom-call.47
  767.9 11.7 %cholesky.188 = f32[128,128]{1,0:T(8,128)S(1)} custom-call(f32[128,128]{1,0:T(8,128)S(1)} %cholesky.428), custom_call_target="Cholesky" | custom-call | tf_op jit(solution)/shard_map/jit(cholesky)/cholesky | solution.py:73
  779.6 10.0 %custom-call.48 = f32[1,128,128]{1,2,0:T(8,128)S(1)} custom-call(f32[1,128,128]{2,1,0:T(8,128)S(1)} %get-tuple-element.42), custom_call_target="InvertDiagBlocksLowerTriangular" | custom-call | tf_op jit(solution)/shard_map/jit(cholesky)/cholesky | solution.py:73
  793.2 11.7 %cholesky.354 = f32[128,128]{1,0:T(8,128)S(1)} custom-call(f32[128,128]{1,0:T(8,128)S(1)} %cholesky.433), custom_call_target="Cholesky" | custom-call | tf_op jit(solution)/shard_map/jit(cholesky)/cholesky | solution.py:73
  805.7 9.8 custom-call.49
  819.0 12.1 %cholesky.373 = f32[128,128]{1,0:T(8,128)S(1)} custom-call(f32[128,128]{1,0:T(8,128)S(1)} %cholesky.438), custom_call_target="Cholesky" | custom-call | tf_op jit(solution)/shard_map/jit(cholesky)/cholesky | solution.py:73
  831.8 9.8 custom-call.50
  844.9 13.2 %cholesky.392 = f32[128,128]{1,0:T(8,128)} custom-call(f32[128,128]{1,0:T(8,128)} %cholesky.443), custom_call_target="Cholesky" | custom-call | tf_op jit(solution)/shard_map/jit(cholesky)/cholesky | solution.py:73
  860.2 11.3 %custom-call.51 = f32[1,128,128]{1,2,0:T(8,128)} custom-call(f32[1,128,128]{2,1,0:T(8,128)} %get-tuple-element.33), custom_call_target="InvertDiagBlocksLowerTriangular" | custom-call | tf_op jit(solution)/shard_map/jit(cholesky)/cholesky | solution.py:73
  873.9 11.9 %cholesky.410 = f32[128,128]{1,0:T(8,128)S(1)} custom-call(f32[128,128]{1,0:T(8,128)S(1)} %convolution_subtract_fusion.8), custom_call_target="Cholesky" | custom-call | tf_op jit(solution)/shard_map/jit(cholesky)/cholesky | solution.py:73
  892.7 21.5 %while.1 = (s32[]{:T(128)}, f32[768,768]{1,0:T(8,128)}, s32[6,2]{0,1:T(2,128)S(1)}, f32[6,128,128]{2,1,0:T(8,128)}, s32[]{:T(128)}) while((s32[]{:T(128)}, f32[768,768]{1,0:T(8,128)}, s32[6,2]{0,1:T(2,128)S(1)}, f32[6,128,128]{2,1,0:T(8,128)}, s32[]{:T(128)}) %tuple.44), condition=%wide.while_cond, body=%wide.while_body.sunk | while | flops 2 | bytes 132705 | solution.py:75
  893.4 3.0 bitcast_dynamic-update-slice_fusion.2
  897.1 2.9 bitcast_dynamic-update-slice_fusion.2
  900.6 2.9 bitcast_dynamic-update-slice_fusion.2
  904.2 2.9 bitcast_dynamic-update-slice_fusion.2
  907.8 2.9 bitcast_dynamic-update-slice_fusion.2
  914.3 60.4 %custom-call.52 = f32[6,128,128]{1,2,0:T(8,128)} custom-call(f32[6,128,128]{2,1,0:T(8,128)} %get-tuple-element.9), custom_call_target="InvertDiagBlocksLowerTriangular" | custom-call | tf_op jit(solution)/shard_map/jit(_solve_triangular)/triangular_solve | solution.py:75
  (115 shorter events, 67.9 us)
Async XLA Ops:
  7.2 100.3 %reduce-scatter.6.cloned.1.call-start = ((), (), s32[]{:S(2)}) async-start(), calls=%async_computation.6 | async-start | bytes 1114112 | tf_op jit(solution)/shard_map/reduce_scatter | solution.py:17
  37.0 165.1 %reduce-scatter.10.cloned.1.call-start = ((), (), s32[]{:S(2)}) async-start(), calls=%async_computation.12 | async-start | bytes 1114112 | tf_op jit(solution)/shard_map/reduce_scatter | solution.py:17
  137.4 159.7 %reduce-scatter.8.cloned.1.call-start = ((), (), s32[]{:S(2)}) async-start(), calls=%async_computation.7 | async-start | bytes 1114112 | tf_op jit(solution)/shard_map/reduce_scatter | solution.py:17
  227.4 69.8 %copy-start.11 = (f32[64,256]{1,0:T(8,128)S(1)}, f32[64,256]{1,0:T(8,128)}, u32[]{:S(2)}) copy-start(f32[64,256]{1,0:T(8,128)} %reduce-scatter.6.cloned.1.call-done) | copy-start | bytes 196612
  227.4 141.2 %copy-start.9 = (bf16[32,1024]{1,0:T(8,128)(2,1)S(1)}, bf16[32,1024]{1,0:T(8,128)(2,1)}, u32[]{:S(2)}) copy-start(bf16[32,1024]{1,0:T(8,128)(2,1)} %param.5) | copy-start | bytes 196612
  232.4 136.1 %all-gather.4.cloned.1.call-start = ((), (), s32[]{:S(2)}) async-start(), calls=%async_computation.8 | async-start | bytes 1114112 | tf_op jit(solution)/shard_map/all_gather | solution.py:29
  233.0 206.2 %all-gather.6.cloned.1.call-start = ((), (), s32[]{:S(2)}) async-start(), calls=%async_computation.9 | async-start | bytes 1114112 | tf_op jit(solution)/shard_map/all_gather | solution.py:30
  298.7 270.2 %all-reduce.3.cloned.1.call-start = ((), (), s32[]{:S(2)}) async-start(), calls=%async_computation.10 | async-start | bytes 196608 | tf_op jit(solution)/shard_map/psum | solution.py:67
  439.2 132.3 %copy-start = (f32[1024,256]{1,0:T(8,128)S(1)}, f32[1024,256]{1,0:T(8,128)}, u32[]{:S(2)}) copy-start(f32[1024,256]{1,0:T(8,128)} %all-gather.6.cloned.1.call-done) | copy-start | bytes 3145732
  441.0 131.6 %copy-start.1 = (bf16[512,1024]{1,0:T(8,128)(2,1)S(1)}, bf16[512,1024]{1,0:T(8,128)(2,1)}, u32[]{:S(2)}) copy-start(bf16[512,1024]{1,0:T(8,128)(2,1)} %all-gather.4.cloned.1.call-done) | copy-start | bytes 3145732
  441.7 293.7 %all-gather.8.cloned.1.call-start = ((), (), s32[]{:S(2)}) async-start(), calls=%async_computation.11 | async-start | bytes 1671168 | tf_op jit(solution)/shard_map/all_gather | solution.py:69
  735.4 1.6 copy-start.5
  741.2 1.4 copy-start.4
  767.1 0.7 copy-start.6
  792.5 0.7 copy-start.7
  818.3 0.7 copy-start.8
  892.7 85.3 %copy-start.3 = (f32[768,768]{1,0:T(8,128)S(1)}, f32[768,768]{1,0:T(8,128)}, u32[]{:S(2)}) copy-start(f32[768,768]{1,0:T(8,128)} %fusion.20) | copy-start | bytes 7077892
  974.7 2.8 copy-start.10
  984.4 3.4 copy-start.2
Sparse Core Ops, SparseCore 0:
  37.2 70.2 reduce-scatter.5
  137.5 64.5 reduce-scatter.9
  232.6 64.5 reduce-scatter.7
  299.3 69.1 all-gather.3
  371.3 67.9 all-gather.5
  443.2 125.5 all-reduce.2
  570.9 71.5 all-gather.7
